TPU v7x, 512 devices: a whole 4x4x16 slice. The times are simulated.
512 devices in a mesh: row: 64 (over z_lo, x, y), col: 8 (over z_hi, core).
Axes of the slice: x: 4, y: 4, z: 16 (z_hi: 4, z_lo: 4; z = z_hi * 4 + z_lo), core: 2. Of those that a mesh axis runs over, the one named last changes fastest.
Arguments:
- latent: bfloat16 [64, 32, 64, 640], P('row', None, 'col')
- stale_rim: bfloat16 [64, 32, 64, 640], P('row', None, 'col'), may hold values from -4 to 4
- stale_kv: bfloat16 [2, 64, 32, 64, 640], P(None, 'row', None, 'col'), may hold values from -96 to 96
- norm_gain: float32 [640], replicated, may hold values from 0.1 to 1.9
- norm_shift: float32 [640], replicated, may hold values from -2 to 2
- conv_weight: bfloat16 [9, 640, 640], P(None, 'row'), may hold values from -0.078125 to 0.078125
- conv_bias: float32 [640], replicated, may hold values from -2.5 to 2.5
- attn_gain: float32 [640], replicated, may hold values from 0.1 to 1.9
- qkv_weight: bfloat16 [640, 1920], P('row'), may hold values from -0.25 to 0.25
Outputs:
- block_out: bfloat16 [64, 32, 64, 640], P('row', None, 'col')
- attended: bfloat16 [64, 32, 64, 640], P('row', None, 'col')
- fresh_kv: bfloat16 [2, 64, 32, 64, 640], P(None, 'row', None, 'col')
All inputs are finite; a program needn't handle non-finite values.
Results may differ from a plain program's by a relative error of at most 0.025.
Values may be sent and summed in bfloat16 or wider, within the bound.
A program may use at most 128 MiB of HBM per device.

v0:
```python
import jax
import jax.numpy as jnp
from jax import lax
from jax.sharding import PartitionSpec as P

HEADS = 10
HEAD_DIM = 64
GROUPS = 16


EPS = 1e-05


def extended(cells, sides, width):
    for axis, dim in sides:
        count = lax.axis_size(axis)
        ends = count - 1
        head = lax.slice_in_dim(cells, 0, width, axis=dim)
        tail = lax.slice_in_dim(cells, cells.shape[dim] - width, cells.shape[dim], axis=dim)
        cells = jnp.concatenate(
            [
                lax.ppermute(tail, axis, [(i, (i + 1) % count) for i in range(ends)]),
                cells,
                lax.ppermute(head, axis, [((i + 1) % count, i) for i in range(ends)]),
            ],
            axis=dim,
        )
    return cells


def on_device(
    latent,
    stale_rim,
    stale_kv,
    norm_gain,
    norm_shift,
    conv_weight,
    conv_bias,
    attn_gain,
    qkv_weight,
):
    images, row_count, strip_cols, width = latent.shape
    tokens_count = images * row_count * strip_cols
    strips = lax.axis_size("col")
    tokens = latent.reshape(tokens_count, width).astype(jnp.float32)
    grouped = tokens.reshape(images, row_count * strip_cols, GROUPS, width // GROUPS)
    first, second = lax.psum(
        (jnp.sum(grouped, axis=(1, 3)), jnp.sum(grouped * grouped, axis=(1, 3))), "col"
    )
    count = row_count * strip_cols * strips * (width // GROUPS)
    average = first / count
    spread = second / count - average * average
    normed_group = (grouped - average[:, None, :, None]) * lax.rsqrt(spread + EPS)[:, None, :, None]
    normed_group = (
        normed_group.reshape(images, row_count, strip_cols, width) * norm_gain + norm_shift
    )
    fresh = jax.nn.silu(normed_group).astype(jnp.bfloat16)
    rimmed = extended(stale_rim, (("col", 2),), 1)
    rimmed = rimmed.at[:, :, 1:-1].set(fresh)
    padded = jnp.pad(rimmed, ((0, 0), (1, 1), (0, 0), (0, 0)))
    windows = jnp.stack(
        [
            padded[:, tap_row : tap_row + row_count, tap_col : tap_col + strip_cols].reshape(
                tokens_count, width
            )
            for tap_row in range(3)
            for tap_col in range(3)
        ]
    )
    channel_part = windows
    summed = jnp.einsum(
        "tqc,tco->qo",
        channel_part,
        lax.all_gather(conv_weight, "row", axis=1, tiled=True),
        preferred_element_type=jnp.float32,
    )
    block = (tokens + summed + conv_bias).astype(jnp.bfloat16)
    rows_float = block.astype(jnp.float32)
    row_mean = jnp.mean(rows_float, axis=1, keepdims=True)
    centered = rows_float - row_mean
    row_var = jnp.mean(centered * centered, axis=1, keepdims=True)
    normed = (centered * lax.rsqrt(row_var + EPS) * attn_gain).astype(jnp.bfloat16)
    channel_part = normed
    projected = jnp.dot(
        channel_part,
        lax.all_gather(qkv_weight, "row", axis=0, tiled=True),
        preferred_element_type=jnp.float32,
    ).astype(jnp.bfloat16)
    queries = projected[:, :width].reshape(tokens_count, HEADS, HEAD_DIM)
    new_keys = projected[:, width : 2 * width]
    new_values = projected[:, 2 * width :]
    fresh_kv = jnp.stack([new_keys, new_values]).reshape(2, images, row_count, strip_cols, width)
    factor = HEAD_DIM ** (-0.5)
    my_strip = lax.axis_index("col")
    score_new = (
        jnp.einsum(
            "qhd,khd->hqk",
            queries,
            new_keys.reshape(tokens_count, HEADS, HEAD_DIM),
            preferred_element_type=jnp.float32,
        )
        * factor
    )
    top_init = jnp.max(score_new, axis=2)
    weight_new = jnp.exp(score_new - top_init[:, :, None])
    total_init = jnp.sum(weight_new, axis=2)
    accum_init = jnp.einsum(
        "hqk,khd->hqd",
        weight_new.astype(jnp.bfloat16),
        new_values.reshape(tokens_count, HEADS, HEAD_DIM),
        preferred_element_type=jnp.float32,
    )

    def one_block(state, item):
        top, total, accum = state
        block_keys, block_values, block_mask = item
        scores = (
            jnp.einsum("qhd,khd->hqk", queries, block_keys, preferred_element_type=jnp.float32)
            * factor
        )
        scores = jnp.where(block_mask[None, None, :], -jnp.inf, scores)
        new_top = jnp.maximum(top, jnp.max(scores, axis=2))
        rescale = jnp.exp(top - new_top)
        weights = jnp.exp(scores - new_top[:, :, None])
        total = total * rescale + jnp.sum(weights, axis=2)
        accum = accum * rescale[:, :, None] + jnp.einsum(
            "hqk,khd->hqd",
            weights.astype(jnp.bfloat16),
            block_values,
            preferred_element_type=jnp.float32,
        )
        return ((new_top, total, accum), None)

    piece = lax.all_gather(stale_kv, "col", axis=3, tiled=True)
    piece_cols = piece.shape[3]
    length = piece.shape[1] * piece.shape[2] * piece_cols
    block_size = min(length, 512)
    blocks = -(-length // block_size)
    cell_ids = jnp.arange(blocks * block_size, dtype=jnp.int32)
    column = cell_ids % piece_cols
    masked = (column // strip_cols == my_strip) | (cell_ids >= length)
    flat = piece.reshape(2, length, width)
    key_blocks = flat[0].reshape(blocks, block_size, HEADS, HEAD_DIM)
    value_blocks = flat[1].reshape(blocks, block_size, HEADS, HEAD_DIM)
    mask_blocks = masked.reshape(blocks, block_size)
    state, _ = lax.scan(
        one_block, (top_init, total_init, accum_init), (key_blocks, value_blocks, mask_blocks)
    )
    top, total, accum = state
    result = accum / total[:, :, None]
    attended = (
        result.transpose(1, 0, 2)
        .reshape(tokens_count, width)
        .astype(jnp.bfloat16)
        .reshape(images, row_count, strip_cols, width)
    )
    return (block.reshape(images, row_count, strip_cols, width), attended, fresh_kv)


def solution(mesh):
    return jax.shard_map(
        on_device,
        mesh=mesh,
        in_specs=(
            P("row", None, "col", None),
            P("row", None, "col", None),
            P(None, "row", None, "col", None),
            P(),
            P(),
            P(None, "row", None),
            P(),
            P(),
            P("row", None),
        ),
        out_specs=(
            P("row", None, "col", None),
            P("row", None, "col", None),
            P(None, "row", None, "col", None),
        ),
        check_vma=False,
    )
```

profile of v0, /device:TPU:8, one launch (start us, length us, event | category | flops | bytes accessed | tf_op | source)
XLA Modules:
  0.0 916.1 jit_solution(16882704505068688075)
XLA Ops:
  7.2 0.7 all-gather.9.cloned.1.call-update
  8.0 0.7 all-gather.7.cloned.1.call-update
  8.7 1.6 copy.42
  10.4 1.2 fusion.80
  11.6 1.7 collective-permute-start
  13.3 1.3 collective-permute-start.1
  14.6 1.1 convert_reduce_fusion
  15.9 0.1 reduce_sum.74
  16.0 0.1 reduce_sum.78
  16.1 29.6 %all-reduce.1 = (f32[1,16]{1,0:T(1,128)S(1)}, f32[1,16]{1,0:T(1,128)S(1)}) all-reduce(f32[1,16]{1,0:T(1,128)S(1)} %bitcast.112, f32[1,16]{1,0:T(1,128)S(1)} %bitcast.111), channel_id=1, replica_groups=mesh['row'=64,'col'=8] {'col'}, use_global_device_ids=true, to_apply=%region_5.6 | all-reduce | flops 32 | bytes 256 | tf_op jit(solution)/shard_map/psum | solution.py:47
  45.8 0.1 mul.87
  46.0 0.1 sub.56
  46.1 1.3 fusion.51
  47.5 0.4 pad_maximum_fusion
  47.8 3.8 scatter.4
  51.7 0.8 fusion.54
  52.4 0.8 fusion.56
  53.3 0.8 fusion.58
  54.1 0.8 fusion.67
  54.9 1.0 bitcast_dynamic-update-slice_fusion
  55.9 0.8 fusion.66
  56.7 0.7 fusion.60
  57.4 0.8 fusion.62
  58.3 0.9 fusion.64
  59.2 312.8 %all-gather.9.cloned.1.call-done = bf16[64,10,1920]{2,1,0:T(8,128)(2,1)} async-done(((bf16[1,10,1920]{2,1,0:T(8,128)(2,1)}), bf16[64,10,1920]{2,1,0:T(8,128)(2,1)}) %all-gather.9.cloned.1.call-update) | async-done | bytes 2457616 | tf_op jit(solution)/shard_map/all_gather | solution.py:86
  372.0 5.4 reshape.153
  377.4 109.2 %all-gather.7.cloned.1.call-done = bf16[2,1,32,64,640]{4,3,2,1,0:T(8,128)(2,1)} async-done(((bf16[2,1,32,8,640]{4,3,2,1,0:T(8,128)(2,1)}), bf16[2,1,32,64,640]{4,3,2,1,0:T(8,128)(2,1)}) %all-gather.7.cloned.1.call-update) | async-done | bytes 5242896 | tf_op jit(solution)/shard_map/all_gather | solution.py:134
  486.6 4.5 fusion.79
  491.1 6.7 reshape.155
  497.8 7.8 copy.50
  505.7 10.2 %reshape.156 = bf16[4,512,10,64]{3,2,1,0:T(8,128)(2,1)} reshape(bf16[1,1,32,64,640]{4,3,2,1,0:T(8,128)(2,1)} %get-tuple-element.116) | data formatting | bytes 5242880 | tf_op jit(solution)/shard_map/reshape;squeeze | solution.py:144
  515.8 9.0 copy.51
  524.9 337.8 %all-gather.5.cloned.1.call-done = bf16[9,640,640]{2,0,1:T(8,128)(2,1)} async-done(((bf16[9,10,640]{2,0,1:T(8,128)(2,1)}), bf16[9,640,640]{2,0,1:T(8,128)(2,1)}) %all-gather.5.cloned.1.call-update) | async-done | bytes 7372816 | tf_op jit(solution)/shard_map/all_gather | solution.py:74
  862.7 8.8 convert_reduce_fusion.1
  871.5 0.2 fusion.40
  871.7 1.1 convolution_convert_fusion
  872.8 1.1 slice_bitcast_fusion.3
  873.9 1.1 copy.44
  875.0 1.9 copy.45
  876.9 1.9 copy.46
  878.8 1.6 multiply_reduce_fusion
  880.4 0.4 fusion.21
  880.8 1.4 fusion.22
  882.2 22.9 %while.15 = (s32[]{:T(128)}, f32[10,256]{1,0:T(8,128)S(1)}, f32[10,256]{1,0:T(8,128)S(1)}, f32[10,256,64]{1,2,0:T(8,128)}, pred[4,512]{1,0:T(4,128)(4,1)S(1)}, /...) while((s32[]{:T(128)}, f32[10,256]{1,0:T(8,128)S(1)}, ...), condition=%wide.region_13.14_spmd, body=%wide.region_10.13_spmd.sunk | while | flops 350295040 | bytes 24087708 | solution.py:146
  882.3 1.2 bitcast_reduce_fusion.2
  883.5 1.1 fusion.95
  884.7 2.5 fusion.96
  887.2 0.8 copy-done.2
  888.0 1.2 bitcast_reduce_fusion.2
  889.2 1.1 fusion.95
  890.4 2.5 fusion.96
  892.9 0.8 copy-done.2
  893.7 1.2 bitcast_reduce_fusion.2
  895.0 1.1 fusion.95
  896.1 2.5 fusion.96
  898.6 0.8 copy-done.2
  899.5 1.2 bitcast_reduce_fusion.2
  900.7 1.1 fusion.95
  901.9 2.5 fusion.96
  904.4 0.8 copy-done.2
  905.2 1.2 fusion.71
  906.4 0.9 copy.52
  907.3 1.3 convert_element_type.69
  908.6 0.9 pad_maximum_fusion.1
  (62 shorter events, 0.8 us)
Async XLA Ops:
  7.2 40.3 %copy-start.6 = (bf16[1,32,8,640]{3,2,1,0:T(8,128)(2,1)S(1)}, bf16[1,32,8,640]{3,2,1,0:T(8,128)(2,1)}, u32[]{:S(2)}) copy-start(bf16[1,32,8,640]{3,2,1,0:T(8,128)(2,1)} %param.14) | copy-start | bytes 983044
  7.2 364.8 %all-gather.9.cloned.1.call-start = ((), (), s32[]{:S(2)}) async-start(), calls=%async_computation.2 | async-start | bytes 3993600 | tf_op jit(solution)/shard_map/all_gather | solution.py:86
  7.9 478.6 %all-gather.7.cloned.1.call-start = ((), (), s32[]{:S(2)}) async-start(), calls=%async_computation.1 | async-start | bytes 5898240 | tf_op jit(solution)/shard_map/all_gather | solution.py:134
  8.7 854.0 %all-gather.5.cloned.1.call-start = ((), (), s32[]{:S(2)}) async-start(), calls=%async_computation | async-start | bytes 13312000 | tf_op jit(solution)/shard_map/all_gather | solution.py:74
  11.6 35.9 %collective-permute-start = (bf16[1,32,1,640]{3,2,1,0:T(2,128)(2,1)S(1)}, bf16[1,32,1,640]{3,2,1,0:T(2,128)(2,1)S(1)}, u32[]{:S(2)}, u32[]{:S(2)}) collective-permute-start(bf16[1,32,1,640]{3,2,1,0:T(2,128)(2,1)S(1)} %get-tuple-element.123), channel_id=1, source_target_pairs={{0,1},{1,2},{2,3},{3,4},{4,5},{5,6},{6,7},{8,9},{9,10},{10,11},{11... | collective-permute-start | bytes 122888 | tf_op jit(solution)/shard_map/ppermute | solution.py:22
  13.3 34.1 %collective-permute-start.1 = (bf16[1,32,1,640]{3,2,1,0:T(2,128)(2,1)S(1)}, bf16[1,32,1,640]{3,2,1,0:T(2,128)(2,1)S(1)}, u32[]{:S(2)}, u32[]{:S(2)}) collective-permute-start(bf16[1,32,1,640]{3,2,1,0:T(2,128)(2,1)S(1)} %get-tuple-element.124), channel_id=1, source_target_pairs={{1,0},{2,1},{3,2},{4,3},{5,4},{6,5},{7,6},{9,8},{10,9},{11,10},{12... | collective-permute-start | bytes 122888 | tf_op jit(solution)/shard_map/ppermute | solution.py:24
  46.1 8.8 copy-start
  46.1 8.8 copy-start.8
  46.1 8.8 copy-start.9
  515.8 346.8 %copy-start.10 = (f32[640]{0:T(1024)S(1)}, f32[640]{0:T(1024)}, u32[]{:S(2)}) copy-start(f32[640]{0:T(1024)} %param.19) | copy-start | bytes 7684
  524.9 346.8 %copy-start.11 = (f32[640]{0:T(1024)S(1)}, f32[640]{0:T(1024)}, u32[]{:S(2)}) copy-start(f32[640]{0:T(1024)} %param.20) | copy-start | bytes 7684
  862.7 9.1 copy-start.3
  871.4 2.5 copy-start.7
  878.8 2.0 copy-start.5
  883.5 1.2 copy-start.1
  887.1 0.8 copy-start.2
  889.2 1.2 copy-start.1
  892.9 0.8 copy-start.2
  894.9 1.2 copy-start.1
  898.6 0.8 copy-start.2
  900.7 1.2 copy-start.1
  904.3 0.8 copy-start.2
  905.2 3.4 copy-start.4
Sparse Core Ops, SparseCore 0:
  10.1 361.8 all-gather.8
  374.1 112.4 all-gather.6
  489.2 373.3 all-gather.4
where the time goes:
time: 917 us; the launch traced here: 916 us
  waiting for transfers between devices  761 us (83%)
  local copies, waits for them, and re-layouts  69.1 us (8%)
  blocking collectives  29.6 us (3%)
  matrix products  27.4 us (3%)
  between operations  14 us (2%)
  other arithmetic  11.3 us (1%)
    all_gather x1, waiting for transfers between devices, on_device(): lax.all_gather(conv_weight, 'row', axis=1, tiled=True)  338 us
    all_gather x1, waiting for transfers between devices, on_device(): lax.all_gather(qkv_weight, 'row', axis=0, tiled=True)  313 us
    all_gather x1, waiting for transfers between devices, on_device(): piece = lax.all_gather(stale_kv, 'col', axis=3, tiled=True)  109 us
    psum x1, blocking collectives, on_device(): lax.psum((jnp.sum(grouped, axis=(1, 3)), jnp.sum(grouped * grouped, axis=...  29.6 us
  transfers between devices with their start and end apart: 5, of which 3 were waited for; matrix products, arithmetic and copies ran while one was open for 7% of the time, Pallas kernels for 0%

commit v1 on v0

v1 whole, which is shorter than its diff:
```python
import jax
import jax.numpy as jnp
from jax import lax
from jax.experimental import pallas as pl
from jax.experimental.pallas import tpu as pltpu
from jax.sharding import PartitionSpec as P

HEADS = 10
HEAD_DIM = 64
GROUPS = 16
C = 640
ROWS = 32
COLS = 8
T = ROWS * COLS
STRIPS = 8
SHARD = 10
SHARDS = 64
PAIRS = 5
EPS = 1e-05
LOG2E = 1.4426950408889634
MESH = pl.DeviceIdType.MESH
F32 = jnp.float32
BF16 = jnp.bfloat16


def iota(shape, dim):
    return lax.broadcasted_iota(jnp.int32, shape, dim)


def kernel(
    lat_ref, rim_ref, kv_ref, gain_ref, shift_ref, w_ref, bias_ref, again_ref,
    block_ref, att_ref, fkv_ref,
    wg, kvg, stats, edges, halo, packed, conv_acc, wq, q2, top, total, accum,
    sems, arr_wz, arr_wa, arr_wb, arr_ws, arr_st, arr_h, arr_k, arr_kf, arr_ks,
):
    row, col = lax.axis_index("row"), lax.axis_index("col")
    zl, xy = lax.div(row, 16), lax.rem(row, 16)
    x, y = lax.div(xy, 4), lax.rem(xy, 4)
    zh, core = lax.div(col, 2), lax.rem(col, 2)
    a, b = x + core * (y - x), y + core * (x - y)
    sa, sb = 4 - 3 * core, 1 + 3 * core

    def ring(value, size):
        return lax.rem(value + size, size)

    def at_a(step):
        return (zl * 16 + ring(a + step, 4) * sa + b * sb, col)

    def at_b(step):
        return (zl * 16 + a * sa + ring(b + step, 4) * sb, col)

    def at_z(step):
        z = ring(zh * 4 + zl + step, 16)
        return (lax.rem(z, 4) * 16 + xy, lax.div(z, 4) * 2 + core)

    def at_zh(step):
        return (row, ring(zh + step, 4) * 2 + core)

    def at_col(step):
        return (row, ring(col + step, 8))

    sibling = (row, col + 1 - 2 * core)
    cross = at_col(2 * core - 1)

    barrier = pltpu.get_barrier_semaphore()
    partners = [at_a(1), at_a(-1), at_b(1), at_b(-1), at_z(1), at_z(-1)]
    partners += [at_zh(1), at_zh(-1), at_zh(2), sibling, cross]
    for partner in partners:
        pl.semaphore_signal(barrier, inc=1, device_id=partner, device_id_type=MESH)

    sent = []

    def copy(src, dst, arrived, device):
        return pltpu.make_async_remote_copy(
            src_ref=src, dst_ref=dst, send_sem=sems.at[len(sent)], recv_sem=arrived,
            device_id=device, device_id_type=MESH,
        )

    def send(src, dst, arrived, device):
        started = copy(src, dst, arrived, device)
        started.start()
        sent.append(started)

    def landed(dst, arrived):
        pltpu.make_async_remote_copy(
            src_ref=dst, dst_ref=dst, send_sem=sems.at[0], recv_sem=arrived,
            device_id=sibling, device_id_type=MESH,
        ).wait_recv()

    half = pl.ds(2 * core, 2)

    wg[half, pl.ds(row, 1)] = w_ref[half][:, None]
    rim = rim_ref[...].astype(F32)
    edges[0] = rim[:, 0, :].astype(BF16)
    edges[1] = rim[:, COLS - 1, :].astype(BF16)
    latent = lat_ref[...].astype(F32).reshape(T, C)
    first = jnp.sum(latent, axis=0, keepdims=True)
    second = jnp.sum(latent * latent, axis=0, keepdims=True)
    spot = iota((8, C), 0)
    stats[0] = jnp.where(spot == 0, first, jnp.where(spot == 1, second, 0.0))

    pl.semaphore_wait(barrier, len(partners))

    def shard(q, ia, ib):
        return wg.at[half, ring(q, 4) * 16 + ring(ia, 4) * sa + ring(ib, 4) * sb]

    def z_send(dq, step, slot):
        piece = shard(zl + dq, a, b)
        send(piece, piece, arr_wz.at[slot], at_z(step))

    def z_landed(dq, slot):
        landed(shard(zl + dq, a, b), arr_wz.at[slot])

    def a_send(dq, da, step, slot):
        piece = shard(zl + dq, a + da, b)
        send(piece, piece, arr_wa.at[dq, slot], at_a(step))

    def a_landed(dq, da, slot):
        landed(shard(zl + dq, a + da, b), arr_wa.at[dq, slot])

    def b_send(dq, da, db, step, slot):
        piece = shard(zl + dq, a + da, b + db)
        send(piece, piece, arr_wb.at[dq, da, slot], at_b(step))

    def b_landed(dq, da, db, slot):
        landed(shard(zl + dq, a + da, b + db), arr_wb.at[dq, da, slot])

    def spread(dq, da):
        b_send(dq, da, 0, 1, 0)
        b_send(dq, da, 0, -1, 1)

    def spread_on(dq, da):
        b_landed(dq, da, -1, 0)
        b_landed(dq, da, 1, 1)
        if (dq + da) % 2:
            b_send(dq, da, 1, -1, 2)
        else:
            b_send(dq, da, -1, 1, 2)

    def begin(dq):
        a_send(dq, 0, 1, 0)
        a_send(dq, 0, -1, 1)
        spread(dq, 0)

    def second_step(dq):
        a_landed(dq, 3, 0)
        a_landed(dq, 1, 1)
        if dq % 2:
            a_send(dq, 1, -1, 2)
        else:
            a_send(dq, 3, 1, 2)
        spread(dq, 3)
        spread(dq, 1)

    def third_step(dq):
        a_landed(dq, 2, 2)
        spread(dq, 2)

    send(stats.at[0], stats.at[1], arr_st.at[0], sibling)
    z_send(0, 1, 0)
    z_send(0, -1, 1)
    begin(0)
    send(edges.at[1], halo.at[0], arr_h.at[0], at_col(1))
    send(edges.at[0], halo.at[1], arr_h.at[1], at_col(-1))

    def strip(dz, mine, kv, part):
        slot = ring(zh + dz, 4) * 2 + (core if mine else 1 - core)
        return kvg.at[slot, kv, pl.ds(part * (T // 2), T // 2)]

    def own(kv, part):
        return kv_ref.at[kv, pl.ds(part * (T // 2), T // 2)]

    for kv in range(2):
        for part in range(2):
            send(own(kv, part), strip(0, True, kv, part), arr_k.at[0, kv, part], at_zh(1))
            send(own(1 - kv, part), strip(0, True, 1 - kv, part), arr_k.at[1, 1 - kv, part], at_zh(-1))
    for kv in range(2):
        for part in range(2):
            send(own(kv, part), strip(0, True, kv, part), arr_ks.at[0, kv, part], sibling)

    landed(stats.at[1], arr_st.at[0])
    stats[2] = stats[0] + stats[1]
    send(stats.at[2], stats.at[3], arr_st.at[1], at_zh(1))
    send(stats.at[2], stats.at[4], arr_st.at[2], at_zh(-1))
    send(stats.at[2], stats.at[5], arr_st.at[3], at_zh(2))

    second_step(0)
    z_landed(3, 0)
    z_landed(1, 1)

    @pl.when(core == 0)
    def _():
        piece = shard(zl + 1, a, b)
        copy(piece, piece, arr_wz.at[2], at_z(-1)).start()

    @pl.when(core == 1)
    def _():
        piece = shard(zl + 3, a, b)
        copy(piece, piece, arr_wz.at[2], at_z(1)).start()

    sent.append(copy(shard(zl + 1, a, b), shard(zl + 1, a, b), arr_wz.at[2], at_z(1)))
    begin(3)
    begin(1)
    third_step(0)
    z_landed(2, 2)
    begin(2)

    for slot in range(3):
        landed(stats.at[3 + slot], arr_st.at[1 + slot])
    sums = (stats[2] + stats[5]) + (stats[3] + stats[4])
    member = iota((C, 128), 0) - 40 * iota((C, 128), 1)
    member = jnp.where((member >= 0) & (member < 40), 1.0, 0.0)
    back = iota((128, C), 1) - 40 * iota((128, C), 0)
    back = jnp.where((back >= 0) & (back < 40), 1.0, 0.0)
    exact = lax.Precision.HIGHEST
    grouped = jnp.dot(sums, member, precision=exact, preferred_element_type=F32)
    grouped = jnp.dot(grouped, back, precision=exact, preferred_element_type=F32)
    count = T * STRIPS * (C // GROUPS)
    average = grouped[0:1] / count
    spread_of = grouped[1:2] / count - average * average
    factor = lax.rsqrt(spread_of + EPS)

    spread_on(0, 0)
    second_step(3)
    second_step(1)
    spread_on(0, 3)
    spread_on(0, 1)

    latent = lat_ref[...].astype(F32).reshape(T, C)
    normed = (latent - average) * factor * gain_ref[...] + shift_ref[...]
    fresh = (normed / (1.0 + jnp.exp(-normed))).astype(BF16).astype(F32)

    second_step(2)
    spread_on(3, 0)
    spread_on(1, 0)

    landed(halo.at[0], arr_h.at[0])
    landed(halo.at[1], arr_h.at[1])

    def rim_rows(side, present):
        cells = jnp.where(present, halo[side].astype(F32), 0.0)
        return jnp.broadcast_to(cells[:, None, :], (ROWS, COLS, C)).reshape(T, C)

    place = iota((T, C), 0) % COLS
    left = jnp.where(place == 0, rim_rows(0, col > 0), pltpu.roll(fresh, 1, 0))
    right = jnp.where(place == COLS - 1, rim_rows(1, col < STRIPS - 1), pltpu.roll(fresh, T - 1, 0))
    shifted = [left.astype(BF16), fresh.astype(BF16), right.astype(BF16)]

    third_step(3)
    third_step(1)
    spread_on(0, 2)
    spread_on(2, 0)

    for block in range(4):
        lanes = iota((C, 512), 1)
        within = lanes % 32
        base = (block * 16 + lanes // 32) * SHARD - iota((C, 512), 0)
        part = None
        for tap in range(3):
            inside = (within >= SHARD * tap) & (within < SHARD * (tap + 1))
            chosen = inside & (base + within - SHARD * tap == 0)
            chosen = jnp.where(chosen, 1.0, 0.0).astype(BF16)
            term = jnp.dot(shifted[tap], chosen, preferred_element_type=F32)
            part = term if part is None else part + term
        packed[block] = part.astype(BF16)
        if block == 0:
            third_step(2)
            spread_on(3, 3)
            spread_on(3, 1)
        if block == 1:
            spread_on(1, 3)
            spread_on(1, 1)
        if block == 2:
            spread_on(3, 2)
            spread_on(1, 2)
            spread_on(2, 3)
            spread_on(2, 1)
    spread_on(2, 2)

    def whole(dq, which):
        return wg.at[pl.ds(2 * which, 2), pl.ds(ring(zl + dq, 4) * 16, 16)]

    for dq in (0, 3, 1, 2):
        for da in range(4):
            b_landed(dq, da, 2, 2)
        send(whole(dq, core), whole(dq, core), arr_ws.at[dq], sibling)

    for part in range(2):
        landed(strip(-1, True, 0, part), arr_k.at[0, 0, part])
        send(strip(-1, True, 0, part), strip(-1, True, 0, part), arr_kf.at[0, part], at_zh(1))
        send(strip(-1, True, 0, part), strip(-1, True, 0, part), arr_ks.at[1, 0, part], sibling)
        landed(strip(1, True, 1, part), arr_k.at[1, 1, part])
        send(strip(1, True, 1, part), strip(1, True, 1, part), arr_kf.at[1, part], at_zh(-1))
        send(strip(1, True, 1, part), strip(1, True, 1, part), arr_ks.at[2, 1, part], sibling)

    for dq in (0, 3, 1, 2):
        landed(whole(dq, 1 - core), arr_ws.at[dq])

    conv_acc[...] = jnp.zeros_like(conv_acc)

    @pl.loop(0, 4)
    def _(block):
        cells = packed[block]
        for tap in range(3):
            weights = wg[tap, pl.ds(block * 16, 16)].reshape(512, C)
            conv_acc[tap] += jnp.dot(cells, weights, preferred_element_type=F32)

    take = iota((240, 256), 0)
    lanes = iota((240, 256), 1)
    tap_of = jnp.where(take >= 160, 2, jnp.where(take >= 80, 1, 0))
    channel = take - 80 * tap_of
    place = lanes % 32 - SHARD * tap_of
    pick = (place >= 0) & (place < SHARD) & (channel == SHARD * (lanes // 32) + place)
    pick = jnp.where(pick, 1.0, 0.0).astype(BF16)

    @pl.loop(0, 8)
    def _(block):
        part = wg[3, pl.ds(block * 8, 8)].reshape(256, C)
        part = jnp.dot(pick, part, preferred_element_type=F32).astype(BF16)
        for tap in range(3):
            wq[tap, pl.ds(pl.multiple_of(block * 80, 80), 80)] = part[80 * tap : 80 * (tap + 1)]

    blank = jnp.zeros((COLS, C), F32)
    above = jnp.concatenate([blank, conv_acc[0, : T - COLS]], axis=0)
    below = jnp.concatenate([conv_acc[2, COLS:], blank], axis=0)
    latent = lat_ref[...].astype(F32).reshape(T, C)
    block_out = (latent + (above + conv_acc[1] + below) + bias_ref[...]).astype(BF16)
    block_ref[...] = block_out.astype(F32).reshape(ROWS, COLS, C).astype(BF16)
    cells = block_out.astype(F32)
    centered = cells - jnp.mean(cells, axis=1, keepdims=True)
    variance = jnp.mean(centered * centered, axis=1, keepdims=True)
    cells = (centered * lax.rsqrt(variance + EPS) * again_ref[...]).astype(BF16)

    for tap in range(3):
        projected = jnp.dot(cells, wq[tap], preferred_element_type=F32).astype(BF16)
        if tap > 0:
            fkv_ref[tap - 1] = projected.astype(F32).reshape(ROWS, COLS, C).astype(BF16)
            kvg[col, tap - 1] = projected
        else:
            queries = projected.astype(F32) * HEAD_DIM ** -0.5
            low = iota((T, 128), 1) < HEAD_DIM
            for pair in range(PAIRS):
                two = queries[:, pair * 128 : (pair + 1) * 128]
                q2[pair, :T] = jnp.where(low, two, 0.0).astype(BF16)
                q2[pair, T:] = jnp.where(low, 0.0, two).astype(BF16)

    top[...] = jnp.full(top.shape, -1e30, F32)
    total[...] = jnp.zeros_like(total)
    accum[...] = jnp.zeros_like(accum)

    def attend(slot, start, size):
        @pl.loop(0, PAIRS)
        def _(pair):
            lanes = pl.ds(pl.multiple_of(pair * 128, 128), 128)
            keys = kvg[slot, 0, pl.ds(start, size), lanes]
            values = kvg[slot, 1, pl.ds(start, size), lanes]
            scores = lax.dot_general(
                q2[pair], keys, (((1,), (1,)), ((), ())), preferred_element_type=F32
            ) * LOG2E
            old = top[pair]
            new = jnp.maximum(old, jnp.max(scores, axis=1, keepdims=True))
            rescale = jnp.exp2(old - new)
            weights = jnp.exp2(scores - new[:, :1])
            total[pair] = total[pair] * rescale + jnp.sum(weights, axis=1, keepdims=True)
            accum[pair] = accum[pair] * rescale + jnp.dot(
                weights.astype(BF16), values, preferred_element_type=F32
            )
            top[pair] = new

    def position(dz, mine):
        return ring(zh + dz, 4) * 2 + (core if mine else 1 - core)

    attend(col, 0, T)
    for kv in range(2):
        for part in range(2):
            landed(strip(0, False, kv, part), arr_ks.at[0, kv, part])
    attend(position(0, False), 0, T)

    for part in range(2):
        landed(strip(-1, True, 1, part), arr_k.at[0, 1, part])
        send(strip(-1, True, 1, part), strip(-1, True, 1, part), arr_ks.at[1, 1, part], sibling)
        landed(strip(1, True, 0, part), arr_k.at[1, 0, part])
        send(strip(1, True, 0, part), strip(1, True, 0, part), arr_ks.at[2, 0, part], sibling)
    for index, dz in ((1, -1), (2, 1)):
        attend(position(dz, True), 0, T)
    for index, dz in ((1, -1), (2, 1)):
        for kv in range(2):
            for part in range(2):
                landed(strip(dz, False, kv, part), arr_ks.at[index, kv, part])
        attend(position(dz, False), 0, T)
    for part in range(2):
        for kv in range(2):
            landed(strip(2, True, kv, part), arr_kf.at[kv, part])
            send(strip(2, True, kv, part), strip(2, True, kv, part), arr_ks.at[3, kv, part], sibling)
        attend(position(2, True), part * (T // 2), T // 2)
        for kv in range(2):
            landed(strip(2, False, kv, part), arr_ks.at[3, kv, part])
        attend(position(2, False), part * (T // 2), T // 2)

    low = iota((T, 128), 1) < HEAD_DIM
    for pair in range(PAIRS):
        result = accum[pair] / total[pair]
        two = jnp.where(low, result[:T], result[T:])
        att_ref[:, :, pair * 128 : (pair + 1) * 128] = two.reshape(ROWS, COLS, 128).astype(BF16)

    for started in sent:
        started.wait_send()


def on_device(
    latent, stale_rim, stale_kv, norm_gain, norm_shift, conv_weight, conv_bias, attn_gain, qkv_weight
):
    taps = conv_weight.reshape(3, 3 * SHARD, C)
    projections = qkv_weight.reshape(SHARD, 3, C).transpose(1, 0, 2).reshape(1, 3 * SHARD, C)
    weights = jnp.concatenate([taps, projections], axis=0)
    weights = jnp.pad(weights, ((0, 0), (0, 2), (0, 0)))
    vmem = pl.BlockSpec(memory_space=pltpu.VMEM)
    dma = pltpu.SemaphoreType.DMA
    cells = jax.ShapeDtypeStruct((ROWS, COLS, C), BF16)
    block, attended, fresh_kv = pl.pallas_call(
        kernel,
        out_shape=(cells, cells, jax.ShapeDtypeStruct((2, ROWS, COLS, C), BF16)),
        in_specs=[vmem, vmem, pl.BlockSpec(memory_space=pl.ANY)] + [vmem] * 5,
        out_specs=(vmem, vmem, vmem),
        scratch_shapes=[
            pltpu.VMEM((4, SHARDS, 32, C), BF16),
            pltpu.VMEM((STRIPS, 2, T, C), BF16),
            pltpu.VMEM((6, 8, C), F32),
            pltpu.VMEM((2, ROWS, C), BF16),
            pltpu.VMEM((2, ROWS, C), BF16),
            pltpu.VMEM((4, T, 512), BF16),
            pltpu.VMEM((3, T, C), F32),
            pltpu.VMEM((3, C, C), BF16),
            pltpu.VMEM((PAIRS, 2 * T, 128), BF16),
            pltpu.VMEM((PAIRS, 2 * T, 128), F32),
            pltpu.VMEM((PAIRS, 2 * T, 128), F32),
            pltpu.VMEM((PAIRS, 2 * T, 128), F32),
            dma((128,)),
            dma((3,)),
            dma((4, 3)),
            dma((4, 4, 3)),
            dma((4,)),
            dma((4,)),
            dma((2,)),
            dma((2, 2, 2)),
            dma((2, 2)),
            dma((4, 2, 2)),
        ],
        compiler_params=pltpu.CompilerParams(
            collective_id=0, has_side_effects=True, vmem_limit_bytes=56 * 2**20
        ),
    )(
        latent.reshape(ROWS, COLS, C),
        stale_rim.reshape(ROWS, COLS, C),
        stale_kv.reshape(2, T, C),
        norm_gain.reshape(1, C),
        norm_shift.reshape(1, C),
        weights,
        conv_bias.reshape(1, C),
        attn_gain.reshape(1, C),
    )
    shape = latent.shape
    return block.reshape(shape), attended.reshape(shape), fresh_kv.reshape((2,) + shape)


def solution(mesh):
    cells = P("row", None, "col", None)
    pairs = P(None, "row", None, "col", None)
    return jax.shard_map(
        on_device,
        mesh=mesh,
        in_specs=(cells, cells, pairs, P(), P(), P(None, "row", None), P(), P(), P("row", None)),
        out_specs=(cells, cells, pairs),
        check_vma=False,
    )
```

time: 917 us -> 164 us (0.18)
  the two profiles are of different devices: /device:TPU:8 before, /device:TPU:1 now
where the time goes in v1:
time: 164 us; the launch traced here: 163 us
  Pallas kernels  152 us (93%)
  local copies, waits for them, and re-layouts  9.41 us (6%)
    pallas_call x1, Pallas kernels, on_device(): pl.pallas_call(kernel, out_shape=(cells, cells, jax.ShapeDtypeStruct((2,...  152 us
    unnamed x9, local copies, waits for them, and re-layouts  3.38 us

profile of v1, /device:TPU:1, one launch (start us, length us, event | category | flops | bytes accessed | tf_op | source)
XLA Modules:
  0.0 163.3 jit_solution(1224542248783554545)
XLA Ops:
  0.6 0.0 copy-start.2
  0.6 1.3 reshape.48.gain_ref
  1.9 1.3 reshape.49.shift_ref
  3.2 1.3 reshape.53.bias_ref
  4.5 1.3 reshape.54.again_ref
  5.7 0.9 reshape.51
  6.6 0.0 copy-done.2
  6.7 0.7 fusion.2.w_ref
  7.4 152.5 %shard_map.112 = (bf16[32,8,640]{2,1,0:T(8,128)(2,1)}, bf16[32,8,640]{2,1,0:T(8,128)(2,1)}, bf16[2,32,8,640]{3,2,1,0:T(8,128)(2,1)}) custom-call(bf16[32,8,640]{2,1,0:T(8,128)(2,1)} %bitcast.15, bf16[32,8,640]{2,1,0:T(8,128)(2,1)} %bitcast.16, bf16[2,256,640]{2,1,0:T(8,128)(2,1)} %bitcast.11, f32[1,640]{1,0:T(1,128)} %reshape.48.gain_ref, ...), custom_call_target="tpu_custom_call" | custom-call | tf_op jit(solution)/shard_map/pallas_call | solution.py:420
  159.9 0.0 copy-start.1
  159.9 0.0 copy-start
  159.9 1.8 %copy.21 = bf16[1,32,8,640]{3,2,1,0:T(8,128)(2,1)} copy(bf16[1,32,8,640]{3,2,1,0:T(8,128)(2,1)} %bitcast.14) | data formatting | bytes 655360
  161.7 0.0 copy-done.1
  161.7 0.7 copy.22
  162.4 0.0 copy-done
  162.4 0.8 copy.23
  (3 shorter events, 0.1 us)
Async XLA Ops:
  0.6 6.0 %copy-start.2 = (bf16[9,10,640]{2,1,0:T(8,128)(2,1)S(1)}, bf16[9,10,640]{2,1,0:T(8,128)(2,1)}, u32[]{:S(2)}) copy-start(bf16[9,10,640]{2,1,0:T(8,128)(2,1)} %param.14) | copy-start | bytes 345604
  159.9 1.8 %copy-start.1 = (bf16[32,8,640]{2,1,0:T(8,128)(2,1)S(1)}, bf16[32,8,640]{2,1,0:T(8,128)(2,1)}, u32[]{:S(2)}) copy-start(bf16[32,8,640]{2,1,0:T(8,128)(2,1)} %get-tuple-element.7) | copy-start | bytes 983044
  159.9 2.5 %copy-start = (bf16[2,32,8,640]{3,2,1,0:T(8,128)(2,1)S(1)}, bf16[2,32,8,640]{3,2,1,0:T(8,128)(2,1)}, u32[]{:S(2)}) copy-start(bf16[2,32,8,640]{3,2,1,0:T(8,128)(2,1)} %get-tuple-element.8) | copy-start | bytes 1966084

commit v2 on v1

v2 whole, which is shorter than its diff:
```python
import jax
import jax.numpy as jnp
from jax import lax
from jax.experimental import pallas as pl
from jax.experimental.pallas import tpu as pltpu
from jax.sharding import PartitionSpec as P

HEADS = 10
HEAD_DIM = 64
GROUPS = 16
C = 640
ROWS = 32
COLS = 8
T = ROWS * COLS
STRIPS = 8
SHARD = 10
SHARDS = 64
PAIRS = 5
EPS = 1e-05
LOG2E = 1.4426950408889634
MESH = pl.DeviceIdType.MESH
F32 = jnp.float32
BF16 = jnp.bfloat16


def iota(shape, dim):
    return lax.broadcasted_iota(jnp.int32, shape, dim)


def part_of(q, blocks):
    low = iota((T, 128), 1) < HEAD_DIM
    scaled = q.astype(F32) * HEAD_DIM ** -0.5
    found = []
    for head in range(2):
        mine = jnp.where(low, scaled, 0.0) if head == 0 else jnp.where(low, 0.0, scaled)
        mine = mine.astype(BF16)
        scores = [
            lax.dot_general(mine, keys(), (((1,), (1,)), ((), ())), preferred_element_type=F32)
            for keys, _ in blocks
        ]
        best = scores[0]
        for score in scores[1:]:
            best = jnp.maximum(best, score)
        top = jnp.max(best, axis=1, keepdims=True) * LOG2E
        total = result = None
        for score, (_, values) in zip(scores, blocks):
            weights = jnp.exp2(score * LOG2E - top)
            term = jnp.dot(weights.astype(BF16), values(), preferred_element_type=F32)
            total = weights if total is None else total + weights
            result = term if result is None else result + term
        total = jnp.sum(total, axis=1, keepdims=True)
        found.append((result / total, top + jnp.log(total) * LOG2E))
    result = jnp.where(low, found[0][0], found[1][0])
    return result, jnp.where(low, found[0][1], found[1][1])


def kernel(
    lat_ref, rim_ref, kv_ref, gain_ref, shift_ref, w_ref, bias_ref, again_ref,
    block_ref, att_ref, fkv_ref,
    wg, kvp, kv4, stats, edges, halo, packed, conv_acc, wq,
    qs, qin, kf, fresh_o, fresh_l, rout, sout, rin, sin,
    sems, own_sem, arr_wz, arr_wa, arr_wb, arr_ws, arr_st, arr_h,
    arr_p, arr_4, arr_ps, arr_4s, arr_q, arr_r, arr_s,
):
    row, col = lax.axis_index("row"), lax.axis_index("col")
    zl, xy = lax.div(row, 16), lax.rem(row, 16)
    x, y = lax.div(xy, 4), lax.rem(xy, 4)
    zh, core = lax.div(col, 2), lax.rem(col, 2)
    a, b = x + core * (y - x), y + core * (x - y)
    sa, sb = 4 - 3 * core, 1 + 3 * core

    def ring(value, size):
        return lax.rem(value + size, size)

    def at_a(step):
        return (zl * 16 + ring(a + step, 4) * sa + b * sb, col)

    def at_b(step):
        return (zl * 16 + a * sa + ring(b + step, 4) * sb, col)

    def at_z(step):
        z = ring(zh * 4 + zl + step, 16)
        return (lax.rem(z, 4) * 16 + xy, lax.div(z, 4) * 2 + core)

    def at_zh(step):
        return (row, ring(zh + step, 4) * 2 + core)

    def at_col(step):
        return (row, ring(col + step, 8))

    sibling = (row, col + 1 - 2 * core)
    cross = at_col(2 * core - 1)

    barrier = pltpu.get_barrier_semaphore()
    partners = [at_a(1), at_a(-1), at_a(2), at_b(1), at_b(-1), at_z(1), at_z(-1), at_z(4 * core - 2)]
    partners += [at_zh(1), at_zh(-1), at_zh(2), sibling, cross]
    for partner in partners:
        pl.semaphore_signal(barrier, inc=1, device_id=partner, device_id_type=MESH)

    sent = []

    def copy(src, dst, arrived, device, index=None):
        index = len(sent) if index is None else index
        return pltpu.make_async_remote_copy(
            src_ref=src, dst_ref=dst, send_sem=sems.at[index], recv_sem=arrived,
            device_id=device, device_id_type=MESH,
        )

    def send(src, dst, arrived, device):
        started = copy(src, dst, arrived, device)
        started.start()
        sent.append(started)

    def landed(dst, arrived):
        copy(dst, dst, arrived, sibling, 0).wait_recv()

    half = pl.ds(2 * core, 2)

    def lanes_of(pair):
        return pl.ds(pl.multiple_of(pair * 128, 128), 128)

    wg[half, pl.ds(row, 1)] = w_ref[half][:, None]
    rim = rim_ref[...].astype(F32)
    edges[0] = rim[:, 0, :].astype(BF16)
    edges[1] = rim[:, COLS - 1, :].astype(BF16)
    latent = lat_ref[...].astype(F32).reshape(T, C)
    first = jnp.sum(latent, axis=0, keepdims=True)
    second = jnp.sum(latent * latent, axis=0, keepdims=True)
    spot = iota((8, C), 0)
    stats[0] = jnp.where(spot == 0, first, jnp.where(spot == 1, second, 0.0))

    keep = pltpu.make_async_copy(kv_ref.at[:, :, lanes_of(zh)], kvp.at[col], own_sem.at[0])
    keep.start()

    pl.semaphore_wait(barrier, len(partners))

    def shard(q, ia, ib):
        return wg.at[half, ring(q, 4) * 16 + ring(ia, 4) * sa + ring(ib, 4) * sb]

    def z_send(step, slot):
        piece = shard(zl, a, b)
        send(piece, piece, arr_wz.at[slot], at_z(step))

    def z_landed(dq, slot):
        landed(shard(zl + dq, a, b), arr_wz.at[slot])

    def b_send(dq, da, db, step, slot):
        piece = shard(zl + dq, a + da, b + db)
        send(piece, piece, arr_wb.at[dq, da, slot], at_b(step))

    def b_landed(dq, da, db, slot):
        landed(shard(zl + dq, a + da, b + db), arr_wb.at[dq, da, slot])

    def spread(dq, da):
        b_send(dq, da, 0, 1, 0)
        b_send(dq, da, 0, -1, 1)

    def spread_on(dq, da):
        b_landed(dq, da, -1, 0)
        b_landed(dq, da, 1, 1)
        if (dq + da) % 2:
            b_send(dq, da, 1, -1, 2)
        else:
            b_send(dq, da, -1, 1, 2)

    def a_start(dq):
        piece = shard(zl + dq, a, b)
        for slot, step in ((0, 1), (1, -1), (2, 2)):
            send(piece, piece, arr_wa.at[dq, slot], at_a(step))
        spread(dq, 0)

    def a_next(dq):
        for slot, da in ((0, 3), (1, 1)):
            landed(shard(zl + dq, a + da, b), arr_wa.at[dq, slot])
            spread(dq, da)

    def a_last(dq):
        landed(shard(zl + dq, a + 2, b), arr_wa.at[dq, 2])
        spread(dq, 2)

    def whole(dq, which):
        return wg.at[pl.ds(2 * which, 2), pl.ds(ring(zl + dq, 4) * 16, 16)]

    def finish(dq):
        for da in range(4):
            b_landed(dq, da, 2, 2)
        send(whole(dq, core), whole(dq, core), arr_ws.at[dq], sibling)

    def place_of(dz, mine=True):
        return ring(zh + dz, 4) * 2 + (core if mine else 1 - core)

    send(stats.at[0], stats.at[1], arr_st.at[0], sibling)
    z_send(1, 0)
    z_send(-1, 1)
    z_send(2 - 4 * core, 2)
    a_start(0)
    send(edges.at[1], halo.at[0], arr_h.at[0], at_col(1))
    send(edges.at[0], halo.at[1], arr_h.at[1], at_col(-1))

    landed(stats.at[1], arr_st.at[0])
    stats[2] = stats[0] + stats[1]
    send(stats.at[2], stats.at[3], arr_st.at[1], at_zh(1))
    send(stats.at[2], stats.at[4], arr_st.at[2], at_zh(-1))
    send(stats.at[2], stats.at[5], arr_st.at[3], at_zh(2))

    for dz in (1, 3, 2):
        send(kv_ref.at[:, :, lanes_of(ring(zh + dz, 4))], kvp.at[col], arr_p.at[4 - dz], at_zh(dz))
    last = lanes_of(PAIRS - 1)
    for kv in range(2):
        send(kv_ref.at[kv, :, last], kv4.at[col, kv], arr_4.at[3, kv], at_zh(1))
        send(kv_ref.at[1 - kv, :, last], kv4.at[col, 1 - kv], arr_4.at[1, 1 - kv], at_zh(-1))
    send(kv_ref.at[:, :, lanes_of(zh)], kvp.at[col], arr_ps.at[0], sibling)
    send(kv_ref.at[:, :, last], kv4.at[col], arr_4s.at[0], sibling)

    a_next(0)
    z_landed(3, 0)
    a_start(3)
    z_landed(1, 1)
    a_start(1)
    a_last(0)
    z_landed(2, 2)
    a_start(2)
    spread_on(0, 0)

    a_next(3)
    a_next(1)
    spread_on(0, 3)
    spread_on(0, 1)
    for slot in range(3):
        landed(stats.at[3 + slot], arr_st.at[1 + slot])
    sums = (stats[2] + stats[5]) + (stats[3] + stats[4])
    member = iota((C, 128), 0) - 40 * iota((C, 128), 1)
    member = jnp.where((member >= 0) & (member < 40), 1.0, 0.0)
    back = iota((128, C), 1) - 40 * iota((128, C), 0)
    back = jnp.where((back >= 0) & (back < 40), 1.0, 0.0)
    exact = lax.Precision.HIGHEST
    grouped = jnp.dot(sums, member, precision=exact, preferred_element_type=F32)
    grouped = jnp.dot(grouped, back, precision=exact, preferred_element_type=F32)
    count = T * STRIPS * (C // GROUPS)
    average = grouped[0:1] / count
    spread_of = grouped[1:2] / count - average * average
    factor = lax.rsqrt(spread_of + EPS)


    latent = lat_ref[...].astype(F32).reshape(T, C)
    normed = (latent - average) * factor * gain_ref[...].reshape(1, C) + shift_ref[...].reshape(1, C)
    fresh = (normed / (1.0 + jnp.exp(-normed))).astype(BF16).astype(F32)

    a_last(3)
    a_last(1)
    a_next(2)
    spread_on(3, 0)
    spread_on(1, 0)

    landed(halo.at[0], arr_h.at[0])
    landed(halo.at[1], arr_h.at[1])

    def rim_rows(side, present):
        cells = jnp.where(present, halo[side].astype(F32), 0.0)
        return jnp.broadcast_to(cells[:, None, :], (ROWS, COLS, C)).reshape(T, C)

    place = iota((T, C), 0) & (COLS - 1)
    left = jnp.where(place == 0, rim_rows(0, col > 0), pltpu.roll(fresh, 1, 0))
    right = jnp.where(place == COLS - 1, rim_rows(1, col < STRIPS - 1), pltpu.roll(fresh, T - 1, 0))
    shifted = [left.astype(BF16), fresh.astype(BF16), right.astype(BF16)]

    a_last(2)
    spread_on(0, 2)
    spread_on(2, 0)

    for block in range(4):
        lanes = iota((1, 512), 1)
        within = lanes & 31
        channel = 32 * block + SHARD * (lanes >> 5) + within
        cells = slice(128 * block, 128 * block + 256)
        part = None
        for tap in range(3):
            inside = (within >= SHARD * tap) & (within < SHARD * (tap + 1))
            wanted = jnp.where(inside, channel - SHARD * tap, -1)
            chosen = jnp.where(iota((256, 512), 0) == wanted, 1.0, 0.0).astype(BF16)
            term = jnp.dot(shifted[tap][:, cells], chosen, preferred_element_type=F32)
            part = term if part is None else part + term
        packed[block] = part.astype(BF16)
        if block == 0:
            spread_on(3, 3)
            spread_on(3, 1)
            spread_on(1, 3)
            spread_on(1, 1)
        if block == 1:
            spread_on(3, 2)
            spread_on(1, 2)
        if block == 2:
            spread_on(2, 3)
            spread_on(2, 1)
    finish(0)
    spread_on(2, 2)

    take = iota((240, 256), 0)
    lanes = iota((240, 256), 1)
    tap_of = jnp.where(take >= 160, 2, jnp.where(take >= 80, 1, 0))
    channel = take - 80 * tap_of
    place = (lanes & 31) - SHARD * tap_of
    pick = (place >= 0) & (place < SHARD) & (channel == SHARD * (lanes >> 5) + place)
    pick = jnp.where(pick, 1.0, 0.0).astype(BF16)


    conv_acc[...] = jnp.zeros_like(conv_acc)

    def multiply(dq):
        block = ring(zl + dq, 4)
        landed(whole(dq, 1 - core), arr_ws.at[dq])
        cells = packed[block]
        for tap in range(3):
            weights = wg[tap, pl.ds(block * 16, 16)].reshape(512, C)
            conv_acc[tap] += jnp.dot(cells, weights, preferred_element_type=F32)
        for part in range(2):
            rows = wg[3, pl.ds(block * 16 + part * 8, 8)].reshape(256, C)
            rows = jnp.dot(pick, rows, preferred_element_type=F32).astype(BF16)
            start = pl.multiple_of(block * 160 + part * 80, 80)
            for tap in range(3):
                wq[tap, pl.ds(start, 80)] = rows[80 * tap : 80 * (tap + 1)]

    def pass_on(dz):
        landed(kvp.at[place_of(dz)], arr_p.at[dz])
        send(kvp.at[place_of(dz)], kvp.at[place_of(dz)], arr_ps.at[dz], sibling)

    finish(3)
    multiply(0)
    finish(1)
    multiply(3)
    finish(2)
    pass_on(3)
    pass_on(1)
    multiply(1)
    multiply(2)

    blank = jnp.zeros((COLS, C), F32)
    above = jnp.concatenate([blank, conv_acc[0, : T - COLS]], axis=0)
    below = jnp.concatenate([conv_acc[2, COLS:], blank], axis=0)
    latent = lat_ref[...].astype(F32).reshape(T, C)
    block_out = (latent + (above + conv_acc[1] + below) + bias_ref[...].reshape(1, C)).astype(BF16)
    block_ref[...] = block_out.astype(F32).reshape(ROWS, COLS, C).astype(BF16)
    cells = block_out.astype(F32)
    centered = cells - jnp.mean(cells, axis=1, keepdims=True)
    variance = jnp.mean(centered * centered, axis=1, keepdims=True)
    cells = (centered * lax.rsqrt(variance + EPS) * again_ref[...].reshape(1, C).reshape(1, C)).astype(BF16)

    queries = jnp.dot(cells, wq[0], preferred_element_type=F32).astype(BF16)
    for pair in range(PAIRS):
        qs[pair] = queries[:, pair * 128 : (pair + 1) * 128]
    qin[zh] = qs[zh]
    for dz in (2, 1, 3):
        send(qs.at[ring(zh + dz, 4)], qin.at[zh], arr_q.at[zh], at_zh(dz))
    for tap in (1, 2):
        projected = jnp.dot(cells, wq[tap], preferred_element_type=F32).astype(BF16)
        fkv_ref[tap - 1] = projected.astype(F32).reshape(ROWS, COLS, C).astype(BF16)
        kf[tap - 1] = projected

    landed(kv4.at[place_of(3), 0], arr_4.at[3, 0])
    send(kv4.at[place_of(3), 0], kv4.at[place_of(3), 0], arr_4.at[2, 0], at_zh(1))
    landed(kv4.at[place_of(1), 1], arr_4.at[1, 1])
    send(kv4.at[place_of(1), 1], kv4.at[place_of(1), 1], arr_4.at[2, 1], at_zh(-1))
    landed(kv4.at[place_of(3), 1], arr_4.at[3, 1])
    landed(kv4.at[place_of(1), 0], arr_4.at[1, 0])
    for dz in (3, 1):
        send(kv4.at[place_of(dz)], kv4.at[place_of(dz)], arr_4s.at[dz], sibling)
    pass_on(2)
    keep.wait()

    @pl.loop(0, PAIRS - 1)
    def _(pair):
        lanes = lanes_of(pair)
        result, level = part_of(qs[pair], [(lambda: kf[0, :, lanes], lambda: kf[1, :, lanes])])
        fresh_o[pair] = result
        fresh_l[pair] = level

    for dz in range(4):
        landed(kvp.at[place_of(dz, False)], arr_ps.at[dz])

    def strips_but(mine, ref):
        def block(step, kv):
            return lambda: ref[lax.rem(mine + 1 + step, STRIPS), kv]

        return [(block(step, 0), block(step, 1)) for step in range(STRIPS - 1)]

    def give(turn, dz):
        source = ring(zh + dz, 4)
        results = copy(rout.at[source], rin.at[zh], arr_r.at[zh], at_zh(dz), 120 + turn)
        levels = copy(sout.at[source], sin.at[zh], arr_s.at[zh], at_zh(dz), 124 + turn)
        return results, levels

    @pl.loop(0, 4)
    def _(turn):
        dz = jnp.where(turn == 0, 1, jnp.where(turn == 1, 3, jnp.where(turn == 2, 2, 0)))
        source = ring(zh + dz, 4)

        @pl.when(turn < 3)
        def _():
            landed(qin.at[source], arr_q.at[source])

        result, level = part_of(qin[source], strips_but(source * 2 + core, kvp))
        level = level.T
        level = jnp.where(iota((8, T), 0) == 0, level[0:1], level[HEAD_DIM : HEAD_DIM + 1])

        @pl.when(turn < 3)
        def _():
            rout[source] = result.astype(BF16)
            sout[source] = level
            for outgoing in give(turn, dz):
                outgoing.start()

        @pl.when(turn == 3)
        def _():
            rin[zh] = result.astype(BF16)
            sin[zh] = level

    def put(pair, result):
        att_ref[:, :, pair * 128 : (pair + 1) * 128] = result.reshape(ROWS, COLS, 128).astype(BF16)

    furthest = kv4.at[place_of(2)]
    for kv in range(2):
        landed(kv4.at[place_of(2), kv], arr_4.at[2, kv])
    send(furthest, furthest, arr_4s.at[2], sibling)
    for dz in range(4):
        landed(kv4.at[place_of(dz, False)], arr_4s.at[dz])
    fresh_pair = (lambda: kf[0, :, last], lambda: kf[1, :, last])
    put(PAIRS - 1, part_of(qs[PAIRS - 1], [fresh_pair] + strips_but(col, kv4))[0])

    for dz in (1, 3, 2):
        landed(rin.at[ring(zh + dz, 4)], arr_r.at[ring(zh + dz, 4)])
        landed(sin.at[ring(zh + dz, 4)], arr_s.at[ring(zh + dz, 4)])
    for pair in range(PAIRS - 1):
        level = jnp.where(iota((128, T), 0) < HEAD_DIM, sin[pair, 0:1], sin[pair, 1:2]).T
        most = jnp.maximum(level, fresh_l[pair])
        old, new = jnp.exp2(level - most), jnp.exp2(fresh_l[pair] - most)
        put(pair, (rin[pair].astype(F32) * old + fresh_o[pair] * new) / (old + new))

    for turn, dz in enumerate((1, 3, 2)):
        for outgoing in give(turn, dz):
            outgoing.wait_send()
    for started in sent:
        started.wait_send()


def on_device(
    latent, stale_rim, stale_kv, norm_gain, norm_shift, conv_weight, conv_bias, attn_gain, qkv_weight
):
    taps = conv_weight.reshape(3, 3 * SHARD, C)
    projections = qkv_weight.reshape(SHARD, 3, C).transpose(1, 0, 2).reshape(1, 3 * SHARD, C)
    weights = jnp.concatenate([taps, projections], axis=0)
    weights = jnp.pad(weights, ((0, 0), (0, 2), (0, 0)))
    vmem = pl.BlockSpec(memory_space=pltpu.VMEM)
    dma = pltpu.SemaphoreType.DMA
    cells = jax.ShapeDtypeStruct((ROWS, COLS, C), BF16)
    block, attended, fresh_kv = pl.pallas_call(
        kernel,
        out_shape=(cells, cells, jax.ShapeDtypeStruct((2, ROWS, COLS, C), BF16)),
        in_specs=[vmem, vmem, pl.BlockSpec(memory_space=pl.ANY)] + [vmem] * 5,
        out_specs=(vmem, vmem, vmem),
        scratch_shapes=[
            pltpu.VMEM((4, SHARDS, 32, C), BF16),
            pltpu.VMEM((STRIPS, 2, T, 128), BF16),
            pltpu.VMEM((STRIPS, 2, T, 128), BF16),
            pltpu.VMEM((6, 8, C), F32),
            pltpu.VMEM((2, ROWS, C), BF16),
            pltpu.VMEM((2, ROWS, C), BF16),
            pltpu.VMEM((4, T, 512), BF16),
            pltpu.VMEM((3, T, C), F32),
            pltpu.VMEM((3, C, C), BF16),
            pltpu.VMEM((PAIRS, T, 128), BF16),
            pltpu.VMEM((4, T, 128), BF16),
            pltpu.VMEM((2, T, C), BF16),
            pltpu.VMEM((4, T, 128), F32),
            pltpu.VMEM((4, T, 128), F32),
            pltpu.VMEM((4, T, 128), BF16),
            pltpu.VMEM((4, 8, T), F32),
            pltpu.VMEM((4, T, 128), BF16),
            pltpu.VMEM((4, 8, T), F32),
            dma((128,)),
            dma((1,)),
            dma((3,)),
            dma((4, 3)),
            dma((4, 4, 3)),
            dma((4,)),
            dma((4,)),
            dma((2,)),
            dma((4,)),
            dma((4, 2)),
            dma((4,)),
            dma((4,)),
            dma((4,)),
            dma((4,)),
            dma((4,)),
        ],
        compiler_params=pltpu.CompilerParams(
            collective_id=0, has_side_effects=True, vmem_limit_bytes=56 * 2**20
        ),
    )(
        latent.reshape(ROWS, COLS, C),
        stale_rim.reshape(ROWS, COLS, C),
        stale_kv.reshape(2, T, C),
        norm_gain,
        norm_shift,
        weights,
        conv_bias,
        attn_gain,
    )
    shape = latent.shape
    return block.reshape(shape), attended.reshape(shape), fresh_kv.reshape((2,) + shape)


def solution(mesh):
    cells = P("row", None, "col", None)
    pairs = P(None, "row", None, "col", None)
    return jax.shard_map(
        on_device,
        mesh=mesh,
        in_specs=(cells, cells, pairs, P(), P(), P(None, "row", None), P(), P(), P("row", None)),
        out_specs=(cells, cells, pairs),
        check_vma=False,
    )
```

time: 164 us -> 107 us (0.65)
  the two profiles are of different devices: /device:TPU:1 before, /device:TPU:97 now
where the time goes in v2:
time: 107 us
  Pallas kernels  101 us (94%)
  local copies, waits for them, and re-layouts  4.35 us (4%)
    pallas_call x1, Pallas kernels, on_device(): pl.pallas_call(kernel, out_shape=(cells, cells, jax.ShapeDtypeStruct((2,...  101 us
    unnamed x9, local copies, waits for them, and re-layouts  3.38 us

profile of v2, /device:TPU:97, one launch (start us, length us, event | category | flops | bytes accessed | tf_op | source)
XLA Modules:
  0.0 106.9 jit_solution(1918298495498898159)
XLA Ops:
  0.6 0.0 copy-start.2
  0.6 0.9 reshape.37
  1.6 0.0 copy-done.2
  1.6 0.7 fusion.2.w_ref
  2.3 101.2 %shard_map.112 = (bf16[32,8,640]{2,1,0:T(8,128)(2,1)}, bf16[32,8,640]{2,1,0:T(8,128)(2,1)}, bf16[2,32,8,640]{3,2,1,0:T(8,128)(2,1)}) custom-call(bf16[32,8,640]{2,1,0:T(8,128)(2,1)} %bitcast.15, bf16[32,8,640]{2,1,0:T(8,128)(2,1)} %bitcast.16, bf16[2,256,640]{2,1,0:T(8,128)(2,1)} %bitcast.11, f32[640]{0:T(1024)} %gain_ref.1, f32[640]{0:T(1024)} %shift_ref.1, ...), custom_call_target="tpu_custom_call" | custom-call | tf_op jit(solution)/shard_map/pallas_call | solution.py:455
  103.5 0.0 copy-start.1
  103.5 0.0 copy-start
  103.5 1.8 %copy.21 = bf16[1,32,8,640]{3,2,1,0:T(8,128)(2,1)} copy(bf16[1,32,8,640]{3,2,1,0:T(8,128)(2,1)} %bitcast.14) | data formatting | bytes 655360
  105.3 0.0 copy-done.1
  105.3 0.7 copy.22
  106.1 0.0 copy-done
  106.1 0.8 copy.23
  (3 shorter events, 0.1 us)
Async XLA Ops:
  0.6 1.0 copy-start.2
  103.5 1.8 %copy-start.1 = (bf16[32,8,640]{2,1,0:T(8,128)(2,1)S(1)}, bf16[32,8,640]{2,1,0:T(8,128)(2,1)}, u32[]{:S(2)}) copy-start(bf16[32,8,640]{2,1,0:T(8,128)(2,1)} %get-tuple-element.7) | copy-start | bytes 983044
  103.5 2.5 %copy-start = (bf16[2,32,8,640]{3,2,1,0:T(8,128)(2,1)S(1)}, bf16[2,32,8,640]{3,2,1,0:T(8,128)(2,1)}, u32[]{:S(2)}) copy-start(bf16[2,32,8,640]{3,2,1,0:T(8,128)(2,1)} %get-tuple-element.8) | copy-start | bytes 1966084

commit v3 on v2

--- a/solution.py
+++ b/solution.py
@@ -89,11 +89,10 @@
         return (row, ring(col + step, 8))
 
     sibling = (row, col + 1 - 2 * core)
-    cross = at_col(2 * core - 1)
 
     barrier = pltpu.get_barrier_semaphore()
     partners = [at_a(1), at_a(-1), at_a(2), at_b(1), at_b(-1), at_z(1), at_z(-1), at_z(4 * core - 2)]
-    partners += [at_zh(1), at_zh(-1), at_zh(2), sibling, cross]
+    partners += [at_col(step) for step in range(1, STRIPS)]
     for partner in partners:
         pl.semaphore_signal(barrier, inc=1, device_id=partner, device_id_type=MESH)
 
@@ -127,10 +126,20 @@
     first = jnp.sum(latent, axis=0, keepdims=True)
     second = jnp.sum(latent * latent, axis=0, keepdims=True)
     spot = iota((8, C), 0)
-    stats[0] = jnp.where(spot == 0, first, jnp.where(spot == 1, second, 0.0))
-
-    keep = pltpu.make_async_copy(kv_ref.at[:, :, lanes_of(zh)], kvp.at[col], own_sem.at[0])
-    keep.start()
+    member = iota((C, 128), 0) - 40 * iota((C, 128), 1)
+    member = jnp.where((member >= 0) & (member < 40), 1.0, 0.0)
+    exact = lax.Precision.HIGHEST
+    stats[col] = jnp.dot(
+        jnp.where(spot == 0, first, jnp.where(spot == 1, second, 0.0)), member,
+        precision=exact, preferred_element_type=F32,
+    )
+
+    kept = [
+        pltpu.make_async_copy(kv_ref.at[:, :, lanes_of(ring(zh - which, 4))], kvp.at[which, col], own_sem.at[which])
+        for which in range(2)
+    ]
+    for keep in kept:
+        keep.start()
 
     pl.semaphore_wait(barrier, len(partners))
 
@@ -189,7 +198,8 @@
     def place_of(dz, mine=True):
         return ring(zh + dz, 4) * 2 + (core if mine else 1 - core)
 
-    send(stats.at[0], stats.at[1], arr_st.at[0], sibling)
+    for step in range(1, STRIPS):
+        send(stats.at[col], stats.at[col], arr_st.at[step], at_col(step))
     z_send(1, 0)
     z_send(-1, 1)
     z_send(2 - 4 * core, 2)
@@ -197,19 +207,16 @@
     send(edges.at[1], halo.at[0], arr_h.at[0], at_col(1))
     send(edges.at[0], halo.at[1], arr_h.at[1], at_col(-1))
 
-    landed(stats.at[1], arr_st.at[0])
-    stats[2] = stats[0] + stats[1]
-    send(stats.at[2], stats.at[3], arr_st.at[1], at_zh(1))
-    send(stats.at[2], stats.at[4], arr_st.at[2], at_zh(-1))
-    send(stats.at[2], stats.at[5], arr_st.at[3], at_zh(2))
-
-    for dz in (1, 3, 2):
-        send(kv_ref.at[:, :, lanes_of(ring(zh + dz, 4))], kvp.at[col], arr_p.at[4 - dz], at_zh(dz))
+    def pair_of(dz):
+        return kv_ref.at[:, :, lanes_of(ring(zh + dz, 4))]
+
+    send(pair_of(1), kvp.at[0, col], arr_p.at[0, 3], at_zh(1))
+    send(pair_of(-2), kvp.at[1, col], arr_p.at[1, 1], at_zh(-1))
+    send(pair_of(0), kvp.at[1, col], arr_p.at[1, 3], at_zh(1))
+    send(pair_of(-1), kvp.at[0, col], arr_p.at[0, 1], at_zh(-1))
     last = lanes_of(PAIRS - 1)
-    for kv in range(2):
-        send(kv_ref.at[kv, :, last], kv4.at[col, kv], arr_4.at[3, kv], at_zh(1))
-        send(kv_ref.at[1 - kv, :, last], kv4.at[col, 1 - kv], arr_4.at[1, 1 - kv], at_zh(-1))
-    send(kv_ref.at[:, :, lanes_of(zh)], kvp.at[col], arr_ps.at[0], sibling)
+    send(pair_of(0), kvp.at[0, col], arr_ps.at[0], sibling)
+    send(pair_of(-1), kvp.at[1, col], arr_ps.at[4], sibling)
     send(kv_ref.at[:, :, last], kv4.at[col], arr_4s.at[0], sibling)
 
     a_next(0)
@@ -226,16 +233,14 @@
     a_next(1)
     spread_on(0, 3)
     spread_on(0, 1)
-    for slot in range(3):
-        landed(stats.at[3 + slot], arr_st.at[1 + slot])
-    sums = (stats[2] + stats[5]) + (stats[3] + stats[4])
-    member = iota((C, 128), 0) - 40 * iota((C, 128), 1)
-    member = jnp.where((member >= 0) & (member < 40), 1.0, 0.0)
+    for step in range(1, STRIPS):
+        landed(stats.at[ring(col - step, STRIPS)], arr_st.at[step])
+    sums = stats[0]
+    for strip in range(1, STRIPS):
+        sums = sums + stats[strip]
     back = iota((128, C), 1) - 40 * iota((128, C), 0)
     back = jnp.where((back >= 0) & (back < 40), 1.0, 0.0)
-    exact = lax.Precision.HIGHEST
-    grouped = jnp.dot(sums, member, precision=exact, preferred_element_type=F32)
-    grouped = jnp.dot(grouped, back, precision=exact, preferred_element_type=F32)
+    grouped = jnp.dot(sums, back, precision=exact, preferred_element_type=F32)
     count = T * STRIPS * (C // GROUPS)
     average = grouped[0:1] / count
     spread_of = grouped[1:2] / count - average * average
@@ -320,17 +325,24 @@
             for tap in range(3):
                 wq[tap, pl.ds(start, 80)] = rows[80 * tap : 80 * (tap + 1)]
 
-    def pass_on(dz):
-        landed(kvp.at[place_of(dz)], arr_p.at[dz])
-        send(kvp.at[place_of(dz)], kvp.at[place_of(dz)], arr_ps.at[dz], sibling)
-
+    def arrived(which, dz):
+        landed(kvp.at[which, place_of(dz)], arr_p.at[which, dz])
+
+    def share(dz):
+        strip = kvp.at[:, place_of(dz)]
+        send(strip, strip, arr_ps.at[dz], sibling)
+
+    arrived(0, 3)
+    send(kvp.at[0, place_of(3)], kvp.at[1, place_of(3)], arr_p.at[1, 2], at_zh(1))
+    arrived(1, 1)
+    send(kvp.at[1, place_of(1)], kvp.at[0, place_of(1)], arr_p.at[0, 2], at_zh(-1))
+    send(kv_ref.at[0, :, last], kv4.at[col, 0], arr_4.at[3, 0], at_zh(1))
+    send(kv_ref.at[1, :, last], kv4.at[col, 1], arr_4.at[1, 1], at_zh(-1))
     finish(3)
     multiply(0)
     finish(1)
     multiply(3)
     finish(2)
-    pass_on(3)
-    pass_on(1)
     multiply(1)
     multiply(2)
 
@@ -348,9 +360,12 @@
     queries = jnp.dot(cells, wq[0], preferred_element_type=F32).astype(BF16)
     for pair in range(PAIRS):
         qs[pair] = queries[:, pair * 128 : (pair + 1) * 128]
-    qin[zh] = qs[zh]
-    for dz in (2, 1, 3):
-        send(qs.at[ring(zh + dz, 4)], qin.at[zh], arr_q.at[zh], at_zh(dz))
+    send(qs.at[ring(zh + 1, 4)], qin.at[0], arr_q.at[0], at_zh(1))
+    send(qs.at[ring(zh + 2, 4)], qin.at[1], arr_q.at[1], at_zh(-1))
+    send(kv_ref.at[1, :, last], kv4.at[col, 1], arr_4.at[3, 1], at_zh(1))
+    send(kv_ref.at[0, :, last], kv4.at[col, 0], arr_4.at[1, 0], at_zh(-1))
+    qin[2] = qs[zh]
+    qin[3] = qs[ring(zh - 1, 4)]
     for tap in (1, 2):
         projected = jnp.dot(cells, wq[tap], preferred_element_type=F32).astype(BF16)
         fkv_ref[tap - 1] = projected.astype(F32).reshape(ROWS, COLS, C).astype(BF16)
@@ -360,12 +375,11 @@
     send(kv4.at[place_of(3), 0], kv4.at[place_of(3), 0], arr_4.at[2, 0], at_zh(1))
     landed(kv4.at[place_of(1), 1], arr_4.at[1, 1])
     send(kv4.at[place_of(1), 1], kv4.at[place_of(1), 1], arr_4.at[2, 1], at_zh(-1))
-    landed(kv4.at[place_of(3), 1], arr_4.at[3, 1])
-    landed(kv4.at[place_of(1), 0], arr_4.at[1, 0])
     for dz in (3, 1):
-        send(kv4.at[place_of(dz)], kv4.at[place_of(dz)], arr_4s.at[dz], sibling)
-    pass_on(2)
-    keep.wait()
+        arrived(dz // 3, dz)
+        share(dz)
+    for keep in kept:
+        keep.wait()
 
     @pl.loop(0, PAIRS - 1)
     def _(pair):
@@ -374,8 +388,13 @@
         fresh_o[pair] = result
         fresh_l[pair] = level
 
-    for dz in range(4):
-        landed(kvp.at[place_of(dz, False)], arr_ps.at[dz])
+    for which in range(2):
+        arrived(which, 2)
+    share(2)
+    landed(kvp.at[0, place_of(0, False)], arr_ps.at[0])
+    landed(kvp.at[1, place_of(0, False)], arr_ps.at[4])
+    for dz in (3, 1, 2):
+        landed(kvp.at[:, place_of(dz, False)], arr_ps.at[dz])
 
     def strips_but(mine, ref):
         def block(step, kv):
@@ -383,60 +402,83 @@
 
         return [(block(step, 0), block(step, 1)) for step in range(STRIPS - 1)]
 
-    def give(turn, dz):
-        source = ring(zh + dz, 4)
-        results = copy(rout.at[source], rin.at[zh], arr_r.at[zh], at_zh(dz), 120 + turn)
-        levels = copy(sout.at[source], sin.at[zh], arr_s.at[zh], at_zh(dz), 124 + turn)
+    def give(turn):
+        home, pair = at_zh(3 - 2 * turn), ring(zh - turn, 4)
+        results = copy(rout.at[turn], rin.at[pair], arr_r.at[turn], home, 120 + turn)
+        levels = copy(sout.at[turn], sin.at[pair], arr_s.at[turn], home, 124 + turn)
         return results, levels
 
     @pl.loop(0, 4)
     def _(turn):
-        dz = jnp.where(turn == 0, 1, jnp.where(turn == 1, 3, jnp.where(turn == 2, 2, 0)))
-        source = ring(zh + dz, 4)
-
-        @pl.when(turn < 3)
+        remote = turn < 2
+        which = lax.rem(turn, 2)
+        source = ring(zh + jnp.where(remote, 3 - 2 * turn, 0), 4)
+
+        @pl.when(remote)
         def _():
-            landed(qin.at[source], arr_q.at[source])
-
-        result, level = part_of(qin[source], strips_but(source * 2 + core, kvp))
+            landed(qin.at[turn], arr_q.at[turn])
+
+        result, level = part_of(qin[turn], strips_but(source * 2 + core, kvp.at[which]))
         level = level.T
         level = jnp.where(iota((8, T), 0) == 0, level[0:1], level[HEAD_DIM : HEAD_DIM + 1])
 
-        @pl.when(turn < 3)
+        @pl.when(remote)
         def _():
-            rout[source] = result.astype(BF16)
-            sout[source] = level
-            for outgoing in give(turn, dz):
+            rout[turn] = result.astype(BF16)
+            sout[turn] = level
+            for outgoing in give(turn):
                 outgoing.start()
 
-        @pl.when(turn == 3)
+        @pl.when(turn >= 2)
         def _():
-            rin[zh] = result.astype(BF16)
-            sin[zh] = level
+            pair = ring(zh + 2 - turn, 4)
+            rin[pair] = result.astype(BF16)
+            sin[pair] = level
 
     def put(pair, result):
         att_ref[:, :, pair * 128 : (pair + 1) * 128] = result.reshape(ROWS, COLS, 128).astype(BF16)
 
     furthest = kv4.at[place_of(2)]
+    landed(kv4.at[place_of(3), 1], arr_4.at[3, 1])
+    landed(kv4.at[place_of(1), 0], arr_4.at[1, 0])
+    for dz in (3, 1):
+        send(kv4.at[place_of(dz)], kv4.at[place_of(dz)], arr_4s.at[dz], sibling)
+
+    def strips_at(places):
+        def block(place, kv):
+            return lambda: kv4[place, kv]
+
+        return [(block(place, 0), block(place, 1)) for place in places]
+
+    for dz in (0, 3, 1):
+        landed(kv4.at[place_of(dz, False)], arr_4s.at[dz])
+    near = [(lambda: kf[0, :, last], lambda: kf[1, :, last])]
+    near += strips_at([place_of(0, False)] + [place_of(dz, mine) for dz in (3, 1) for mine in (True, False)])
+    near_o, near_l = part_of(qs[PAIRS - 1], near)
     for kv in range(2):
         landed(kv4.at[place_of(2), kv], arr_4.at[2, kv])
+    furthest = kv4.at[place_of(2)]
     send(furthest, furthest, arr_4s.at[2], sibling)
-    for dz in range(4):
-        landed(kv4.at[place_of(dz, False)], arr_4s.at[dz])
-    fresh_pair = (lambda: kf[0, :, last], lambda: kf[1, :, last])
-    put(PAIRS - 1, part_of(qs[PAIRS - 1], [fresh_pair] + strips_but(col, kv4))[0])
-
-    for dz in (1, 3, 2):
-        landed(rin.at[ring(zh + dz, 4)], arr_r.at[ring(zh + dz, 4)])
-        landed(sin.at[ring(zh + dz, 4)], arr_s.at[ring(zh + dz, 4)])
+    landed(kv4.at[place_of(2, False)], arr_4s.at[2])
+    far_o, far_l = part_of(qs[PAIRS - 1], strips_at([place_of(2), place_of(2, False)]))
+
+    def merged(result, level, other, other_level):
+        most = jnp.maximum(level, other_level)
+        old, new = jnp.exp2(level - most), jnp.exp2(other_level - most)
+        return (result * old + other * new) / (old + new)
+
+    put(PAIRS - 1, merged(near_o, near_l, far_o, far_l))
+
+    for turn in range(2):
+        pair = ring(zh + 1 + turn, 4)
+        landed(rin.at[pair], arr_r.at[turn])
+        landed(sin.at[pair], arr_s.at[turn])
     for pair in range(PAIRS - 1):
         level = jnp.where(iota((128, T), 0) < HEAD_DIM, sin[pair, 0:1], sin[pair, 1:2]).T
-        most = jnp.maximum(level, fresh_l[pair])
-        old, new = jnp.exp2(level - most), jnp.exp2(fresh_l[pair] - most)
-        put(pair, (rin[pair].astype(F32) * old + fresh_o[pair] * new) / (old + new))
-
-    for turn, dz in enumerate((1, 3, 2)):
-        for outgoing in give(turn, dz):
+        put(pair, merged(rin[pair].astype(F32), level, fresh_o[pair], fresh_l[pair]))
+
+    for turn in range(2):
+        for outgoing in give(turn):
             outgoing.wait_send()
     for started in sent:
         started.wait_send()
@@ -459,9 +501,9 @@
         out_specs=(vmem, vmem, vmem),
         scratch_shapes=[
             pltpu.VMEM((4, SHARDS, 32, C), BF16),
+            pltpu.VMEM((2, STRIPS, 2, T, 128), BF16),
             pltpu.VMEM((STRIPS, 2, T, 128), BF16),
-            pltpu.VMEM((STRIPS, 2, T, 128), BF16),
-            pltpu.VMEM((6, 8, C), F32),
+            pltpu.VMEM((STRIPS, 8, 128), F32),
             pltpu.VMEM((2, ROWS, C), BF16),
             pltpu.VMEM((2, ROWS, C), BF16),
             pltpu.VMEM((4, T, 512), BF16),
@@ -472,25 +514,25 @@
             pltpu.VMEM((2, T, C), BF16),
             pltpu.VMEM((4, T, 128), F32),
             pltpu.VMEM((4, T, 128), F32),
-            pltpu.VMEM((4, T, 128), BF16),
-            pltpu.VMEM((4, 8, T), F32),
+            pltpu.VMEM((2, T, 128), BF16),
+            pltpu.VMEM((2, 8, T), F32),
             pltpu.VMEM((4, T, 128), BF16),
             pltpu.VMEM((4, 8, T), F32),
             dma((128,)),
-            dma((1,)),
+            dma((2,)),
             dma((3,)),
             dma((4, 3)),
             dma((4, 4, 3)),
             dma((4,)),
+            dma((STRIPS,)),
+            dma((2,)),
+            dma((2, 4)),
+            dma((4, 2)),
+            dma((5,)),
             dma((4,)),
             dma((2,)),
-            dma((4,)),
-            dma((4, 2)),
-            dma((4,)),
-            dma((4,)),
-            dma((4,)),
-            dma((4,)),
-            dma((4,)),
+            dma((2,)),
+            dma((2,)),
         ],
         compiler_params=pltpu.CompilerParams(
             collective_id=0, has_side_effects=True, vmem_limit_bytes=56 * 2**20

time: 107 us -> 102 us (0.953)
  the two profiles are of different devices: /device:TPU:97 before, /device:TPU:49 now
where the time goes in v3:
time: 102 us
  Pallas kernels  96 us (94%)
  local copies, waits for them, and re-layouts  4.35 us (4%)
    pallas_call x1, Pallas kernels, on_device(): pl.pallas_call(kernel, out_shape=(cells, cells, jax.ShapeDtypeStruct((2,...  96 us
    unnamed x9, local copies, waits for them, and re-layouts  3.38 us

profile of v3, /device:TPU:49, one launch (start us, length us, event | category | flops | bytes accessed | tf_op | source)
XLA Modules:
  0.0 101.7 jit_solution(4682046684882720288)
XLA Ops:
  0.6 0.0 copy-start.2
  0.6 0.9 reshape.37
  1.6 0.0 copy-done.2
  1.6 0.7 fusion.2.w_ref
  2.3 96.0 %shard_map.112 = (bf16[32,8,640]{2,1,0:T(8,128)(2,1)}, bf16[32,8,640]{2,1,0:T(8,128)(2,1)}, bf16[2,32,8,640]{3,2,1,0:T(8,128)(2,1)}) custom-call(bf16[32,8,640]{2,1,0:T(8,128)(2,1)} %bitcast.15, bf16[32,8,640]{2,1,0:T(8,128)(2,1)} %bitcast.16, bf16[2,256,640]{2,1,0:T(8,128)(2,1)} %bitcast.11, f32[640]{0:T(1024)} %gain_ref.1, f32[640]{0:T(1024)} %shift_ref.1, ...), custom_call_target="tpu_custom_call" | custom-call | tf_op jit(solution)/shard_map/pallas_call | solution.py:497
  98.3 0.0 copy-start.1
  98.3 0.0 copy-start
  98.3 1.8 %copy.21 = bf16[1,32,8,640]{3,2,1,0:T(8,128)(2,1)} copy(bf16[1,32,8,640]{3,2,1,0:T(8,128)(2,1)} %bitcast.14) | data formatting | bytes 655360
  100.2 0.0 copy-done.1
  100.2 0.7 copy.22
  100.9 0.0 copy-done
  100.9 0.8 copy.23
  (3 shorter events, 0.1 us)
Async XLA Ops:
  0.6 1.0 copy-start.2
  98.3 1.8 %copy-start.1 = (bf16[32,8,640]{2,1,0:T(8,128)(2,1)S(1)}, bf16[32,8,640]{2,1,0:T(8,128)(2,1)}, u32[]{:S(2)}) copy-start(bf16[32,8,640]{2,1,0:T(8,128)(2,1)} %get-tuple-element.7) | copy-start | bytes 983044
  98.3 2.5 %copy-start = (bf16[2,32,8,640]{3,2,1,0:T(8,128)(2,1)S(1)}, bf16[2,32,8,640]{3,2,1,0:T(8,128)(2,1)}, u32[]{:S(2)}) copy-start(bf16[2,32,8,640]{3,2,1,0:T(8,128)(2,1)} %get-tuple-element.8) | copy-start | bytes 1966084

commit v4 on v3

--- a/solution.py
+++ b/solution.py
@@ -215,6 +215,8 @@
     send(pair_of(0), kvp.at[1, col], arr_p.at[1, 3], at_zh(1))
     send(pair_of(-1), kvp.at[0, col], arr_p.at[0, 1], at_zh(-1))
     last = lanes_of(PAIRS - 1)
+    send(kv_ref.at[0, :, last], kv4.at[col, 0], arr_4.at[3, 0], at_zh(1))
+    send(kv_ref.at[1, :, last], kv4.at[col, 1], arr_4.at[1, 1], at_zh(-1))
     send(pair_of(0), kvp.at[0, col], arr_ps.at[0], sibling)
     send(pair_of(-1), kvp.at[1, col], arr_ps.at[4], sibling)
     send(kv_ref.at[:, :, last], kv4.at[col], arr_4s.at[0], sibling)
@@ -336,8 +338,6 @@
     send(kvp.at[0, place_of(3)], kvp.at[1, place_of(3)], arr_p.at[1, 2], at_zh(1))
     arrived(1, 1)
     send(kvp.at[1, place_of(1)], kvp.at[0, place_of(1)], arr_p.at[0, 2], at_zh(-1))
-    send(kv_ref.at[0, :, last], kv4.at[col, 0], arr_4.at[3, 0], at_zh(1))
-    send(kv_ref.at[1, :, last], kv4.at[col, 1], arr_4.at[1, 1], at_zh(-1))
     finish(3)
     multiply(0)
     finish(1)

time: 102 us -> 101 us (level)
  the two profiles are of different devices: /device:TPU:49 before, /device:TPU:57 now
where the time goes in v4:
time: 101 us; the launch traced here: 100 us
  Pallas kernels  94.6 us (94%)
  local copies, waits for them, and re-layouts  4.35 us (4%)
    pallas_call x1, Pallas kernels, on_device(): pl.pallas_call(kernel, out_shape=(cells, cells, jax.ShapeDtypeStruct((2,...  94.6 us
    unnamed x9, local copies, waits for them, and re-layouts  3.38 us

profile of v4, /device:TPU:57, one launch (start us, length us, event | category | flops | bytes accessed | tf_op | source)
XLA Modules:
  0.0 100.4 jit_solution(2205598106638554645)
XLA Ops:
  0.6 0.0 copy-start.2
  0.6 0.9 reshape.37
  1.6 0.0 copy-done.2
  1.6 0.7 fusion.2.w_ref
  2.3 94.6 %shard_map.112 = (bf16[32,8,640]{2,1,0:T(8,128)(2,1)}, bf16[32,8,640]{2,1,0:T(8,128)(2,1)}, bf16[2,32,8,640]{3,2,1,0:T(8,128)(2,1)}) custom-call(bf16[32,8,640]{2,1,0:T(8,128)(2,1)} %bitcast.15, bf16[32,8,640]{2,1,0:T(8,128)(2,1)} %bitcast.16, bf16[2,256,640]{2,1,0:T(8,128)(2,1)} %bitcast.11, f32[640]{0:T(1024)} %gain_ref.1, f32[640]{0:T(1024)} %shift_ref.1, ...), custom_call_target="tpu_custom_call" | custom-call | tf_op jit(solution)/shard_map/pallas_call | solution.py:497
  97.0 0.0 copy-start.1
  97.0 0.0 copy-start
  97.0 1.8 %copy.21 = bf16[1,32,8,640]{3,2,1,0:T(8,128)(2,1)} copy(bf16[1,32,8,640]{3,2,1,0:T(8,128)(2,1)} %bitcast.14) | data formatting | bytes 655360
  98.8 0.0 copy-done.1
  98.8 0.7 copy.22
  99.5 0.0 copy-done
  99.5 0.8 copy.23
  (3 shorter events, 0.1 us)
Async XLA Ops:
  0.6 1.0 copy-start.2
  97.0 1.8 %copy-start.1 = (bf16[32,8,640]{2,1,0:T(8,128)(2,1)S(1)}, bf16[32,8,640]{2,1,0:T(8,128)(2,1)}, u32[]{:S(2)}) copy-start(bf16[32,8,640]{2,1,0:T(8,128)(2,1)} %get-tuple-element.7) | copy-start | bytes 983044
  97.0 2.5 %copy-start = (bf16[2,32,8,640]{3,2,1,0:T(8,128)(2,1)S(1)}, bf16[2,32,8,640]{3,2,1,0:T(8,128)(2,1)}, u32[]{:S(2)}) copy-start(bf16[2,32,8,640]{3,2,1,0:T(8,128)(2,1)} %get-tuple-element.8) | copy-start | bytes 1966084
